TPU v7x, 32 devices: a whole 2x2x4 slice. The times are simulated.
32 devices in a mesh: lat: 4 (over x, core), lon: 8 (over z, y).
Axes of the slice: x: 2, y: 2, z: 4, core: 2. Of those that a mesh axis runs over, the one named last changes fastest.
Arguments:
- fields: bfloat16 [512, 1440, 256], P('lat', 'lon'), may hold values from -6 to 6
- basis: float32 [512, 4, 3, 17], P('lat'), may hold values from -1 to 1
- reach: int32 [512], P('lat'), may hold values from 1 to 8, as said below
- mixing: bfloat16 [4, 256, 256], replicated, may hold values from -0.1875 to 0.1875
- gains: float32 [2, 720, 256], replicated, may hold values from -5 to 5
Outputs:
- updated: bfloat16 [512, 1440, 256], P('lat', 'lon')
Inputs may be any that keep to these rules, and one draw needn't show every extreme that they name: `reach`: 8 is reached in some row.
All inputs are finite; a program needn't handle non-finite values.
Results may differ from a plain program's by a relative error of at most 0.0062.
Values may be sent and summed in bfloat16 or wider, within the bound.
A program may use at most 576 MiB of HBM per device.

v0:
```python
import jax
import jax.numpy as jnp
from jax import lax
from jax.sharding import PartitionSpec as P

NLON = 1440
MODES = 720
HALO = 8
WIN = 17


def with_halo(block, sides, width, periodic):
    for axis, dim in sides:
        count = lax.axis_size(axis)
        forward = [(i, i + 1) for i in range(count - 1)]
        if periodic:
            forward.append((count - 1, 0))
        backward = [(target, source) for source, target in forward]
        low = lax.ppermute(
            lax.slice_in_dim(block, block.shape[dim] - width, None, axis=dim), axis, forward
        )
        high = lax.ppermute(lax.slice_in_dim(block, 0, width, axis=dim), axis, backward)
        block = jnp.concatenate([low, block, high], axis=dim)
    return block


def make_tables(count, modes):
    index = jnp.arange(count, dtype=jnp.int32)
    wave = jnp.arange(modes, dtype=jnp.int32)
    phase = index[:, None] * wave[None, :] % count
    angle = phase.astype(jnp.float32) * (2.0 * jnp.pi / count)
    cosine = jnp.cos(angle)
    sine = jnp.sin(angle)
    forward = jnp.concatenate([cosine, -sine], 1)
    weights = jnp.where(wave == 0, 1.0, 2.0).astype(jnp.float32) / count
    weights = jnp.concatenate([weights, weights], 0)
    adjoint = forward * weights[None, :]
    return (forward.astype(jnp.bfloat16), adjoint.astype(jnp.bfloat16))


def transform(piece, forward, adjoint, gain_real, gain_imag):
    spectrum = jnp.einsum("rnc,nf->rfc", piece, forward, preferred_element_type=jnp.float32)
    real = spectrum[:, :MODES]
    imag = spectrum[:, MODES:]
    filtered = jnp.concatenate(
        [gain_real * real - gain_imag * imag, gain_real * imag + gain_imag * real], 1
    ).astype(jnp.bfloat16)
    return jnp.einsum("rfc,nf->rnc", filtered, adjoint, preferred_element_type=jnp.float32).astype(
        jnp.bfloat16
    )


def shards(fields, basis, reach, mixing, gains):
    lat_rows, lon_cols, chans = fields.shape
    wide = with_halo(fields, (("lon", 1),), HALO, True)
    padded = with_halo(wide, (("lat", 0),), 1, False)
    offsets = jnp.arange(WIN, dtype=jnp.int32) - HALO
    mask = (jnp.abs(offsets)[None, :] <= reach[:, None]).astype(jnp.float32)
    filters = (basis * mask[:, None, None, :]).astype(jnp.bfloat16)
    target = jnp.arange(lon_cols, dtype=jnp.int32)
    source = jnp.arange(lon_cols + 2 * HALO, dtype=jnp.int32)
    select = (
        source[None, :, None] - target[:, None, None] == offsets[None, None, :] + HALO
    ).astype(jnp.bfloat16)
    band = jnp.einsum(
        "ikab,jpb->ikjap", filters, select, preferred_element_type=jnp.float32
    ).astype(jnp.bfloat16)
    windows = jnp.stack([padded[0:lat_rows], padded[1 : lat_rows + 1], padded[2 : lat_rows + 2]], 1)
    conv = jnp.einsum("ikjap,iapc->ikjc", band, windows, preferred_element_type=jnp.float32).astype(
        jnp.bfloat16
    )
    local = jnp.einsum("ikjc,kcd->ijd", conv, mixing, preferred_element_type=jnp.float32)
    forward, adjoint = make_tables(NLON, MODES)
    gathered = lax.all_to_all(fields, "lon", split_axis=0, concat_axis=1, tiled=True)
    result = transform(gathered, forward, adjoint, gains[0], gains[1])
    back = lax.all_to_all(result, "lon", split_axis=1, concat_axis=0, tiled=True)
    return (fields.astype(jnp.float32) + local + back.astype(jnp.float32)).astype(jnp.bfloat16)


def solution(mesh):
    return jax.shard_map(
        shards,
        mesh=mesh,
        in_specs=(P("lat", "lon", None), P("lat", None, None, None), P("lat"), P(), P()),
        out_specs=P("lat", "lon", None),
        check_vma=False,
    )
```

profile of v0, /device:TPU:13, one launch (start us, length us, event | category | flops | bytes accessed | tf_op | source)
XLA Modules:
  0.0 1040.3 jit_solution(17651418187520683294)
XLA Ops:
  0.0 0.0 copy-start
  0.0 13.9 %copy.26 = bf16[128,180,256]{2,1,0:T(8,128)(2,1)} copy(bf16[128,180,256]{2,0,1:T(8,128)(2,1)} %param.5) | data formatting | bytes 23592960 | tf_op args[0]
  13.9 0.0 copy-start.1
  13.9 5.8 all-to-all-start
  19.7 0.1 pad_maximum_fusion.8
  19.7 0.0 copy-done.1
  19.7 1.0 slice_bitcast_fusion.1
  20.7 19.7 %sine_negate_fusion = (f32[1440,720]{0,1:T(8,128)}, f32[1440,720]{0,1:T(8,128)}) fusion(), kind=kLoop, calls=%fused_computation.40 | loop fusion | flops 10368000 | bytes 8294400 | tf_op jit(solution)/shard_map/neg | solution.py:34
  40.4 0.0 slice-start
  40.4 238.4 %all-to-all-done = bf16[128,180,256]{2,1,0:T(8,128)(2,1)} async-done(((bf16[128,180,256]{2,1,0:T(8,128)(2,1)}), bf16[128,180,256]{2,1,0:T(8,128)(2,1)}, u32[]{:S(2)}, u32[]{:S(2)}) %all-to-all-start) | async-done | bytes 11796512 | tf_op jit(solution)/shard_map/all_to_all | solution.py:74
  278.8 0.0 slice-start.1
  278.8 13.4 %copy.36 = bf16[16,8,180,256]{3,0,2,1:T(8,128)(2,1)S(1)} copy(bf16[16,8,180,256]{3,2,0,1:T(8,128)(2,1)} %bitcast.21) | data formatting | bytes 23592960 | tf_op jit(solution)/shard_map/all_to_all | solution.py:74
  292.2 0.0 slice-done
  292.2 0.0 slice-done.1
  292.2 27.4 %convolution_bitcast_fusion = f32[16,1440,256]{2,1,0:T(8,128)} fusion(bf16[16,1440,256]{2,0,1:T(8,128)(2,1)S(1)} %bitcast.85, f32[1440,720]{0,1:T(8,128)S(1)} %bitcast.87, f32[1440,720]{0,1:T(8,128)} %get-tuple-element.17), kind=kOutput, calls=%fused_computation.13 | convolution fusion | flops 16995225600 | bytes 43683840 | tf_op jit(solution)/shard_map/rnc,nf->rfc/dot_general | solution.py:42
  319.6 14.0 %subtract_convert_fusion = (bf16[16,720,256]{2,1,0:T(8,128)(2,1)}, bf16[16,720,256]{2,1,0:T(8,128)(2,1)}) fusion(f32[16,1440,256]{2,1,0:T(8,128)} %convolution_bitcast_fusion, f32[720,256]{1,0:T(8,128)} %get-tuple-element.15, f32[720,256]{1,0:T(8,128)S(1)} %get-tuple-element.14), kind=kLoop, calls=%fused_computation.29 | loop fusion | flops 23592960 | bytes 36864000 | tf_op jit(solution)/shard_map/convert.3
  333.6 24.8 %fusion.13 = bf16[16,1440,256]{2,1,0:T(8,128)(2,1)S(1)} fusion(bf16[16,720,256]{2,1,0:T(8,128)(2,1)} %get-tuple-element.6, bf16[16,720,256]{2,1,0:T(8,128)(2,1)} %get-tuple-element.5, f32[1440,720]{0,1:T(8,128)} %get-tuple-element.16, f32[1440,720]{0,1:T(8,128)} %get-tuple-element.17, f32[1440]{0:T(1024)S(1)} %pad_maximum_fusion.8), kind=kOutput, calls=%fused_computation.30 | convolution fusion | flops 17022643200 | bytes 31893120 | tf_op jit(solution)/shard_map/rfc,nf->rnc/dot_general | solution.py:48
  358.4 28.1 %copy.39 = bf16[16,1440,256]{2,0,1:T(8,128)(2,1)} copy(bf16[16,1440,256]{2,1,0:T(8,128)(2,1)S(1)} %fusion.13) | data formatting | bytes 23592960 | tf_op jit(solution)/shard_map/convert_element_type | solution.py:48
  386.5 0.0 copy-start.3
  386.5 0.0 copy-start.2
  386.5 7.1 all-to-all-start.1
  393.5 1.5 fusion.41
  395.0 0.3 collective-permute-start.1
  395.4 2.1 collective-permute-start
  397.5 0.0 copy-done.3
  397.5 0.1 compare_convert_fusion
  397.6 0.0 copy-done.2
  397.6 260.3 %collective-permute-done.1 = bf16[128,8,256]{2,1,0:T(8,128)(2,1)S(1)} collective-permute-done((bf16[128,8,256]{2,1,0:T(8,128)(2,1)S(1)}, bf16[128,8,256]{2,1,0:T(8,128)(2,1)S(1)}, u32[]{:S(2)}, u32[]{:S(2)}) %collective-permute-start.1) | collective-permute-done | bytes 524320 | tf_op jit(solution)/shard_map/ppermute | solution.py:22
  657.9 0.1 collective-permute-done
  658.1 7.1 pad_maximum_fusion.6
  665.2 5.6 collective-permute-start.2
  670.8 1.9 collective-permute-start.3
  672.7 39.5 %convert_bitcast_fusion = bf16[128,4,180,3,196]{0,4,3,1,2:T(8,128)(2,1)} fusion(s32[180,196]{1,0:T(8,128)S(1)} %iota_subtract_fusion, bf16[128,4,3,17]{0,1,3,2:T(4,128)(2,1)S(1)} %multiply_convert_fusion.1), kind=kOutput, calls=%fused_computation | convolution fusion | flops 1897252608 | bytes 108573504 | tf_op jit(solution)/shard_map/ikab,jpb->ikjap/dot_general | solution.py:65
  712.2 174.6 %copy.33 = bf16[128,4,180,3,196]{4,2,3,1,0:T(8,128)(2,1)} copy(bf16[128,4,180,3,196]{0,4,3,1,2:T(8,128)(2,1)} %convert_bitcast_fusion) | data formatting | bytes 216760320 | tf_op jit(solution)/shard_map/convert_element_type | solution.py:67
  886.8 0.0 collective-permute-done.2
  886.8 0.0 collective-permute-done.3
  886.8 32.2 %fusion.8 = (bf16[128,1,196,256]{3,2,1,0:T(8,128)(2,1)}, bf16[128,1,196,256]{3,2,1,0:T(8,128)(2,1)}, bf16[128,1,196,256]{3,2,1,0:T(8,128)(2,1)}) fusion(bf16[1,196,256]{2,1,0:T(8,128)(2,1)S(1)} %collective-permute-done.2, bf16[128,8,256]{2,1,0:T(8,128)(2,1)S(1)} %collective-permute-done.1, bf16[128,180,256]{2,1,0:T(8,128)(2,1)} %copy.26, ...), kind=kLoop, calls=%fused_computation.20 | loop fusion | flops 141295616 | bytes 51580928 | tf_op jit(solution)/shard_map/stack | solution.py:68
  919.0 0.0 all-to-all-done.1
  919.0 7.1 convert_bitcast_fusion.1
  926.2 16.6 %copy.40 = f32[8,16,180,256]{3,2,1,0:T(8,128)} copy(f32[8,16,180,256]{3,1,2,0:T(8,128)S(1)} %convert_bitcast_fusion.1) | data formatting | bytes 47185920 | tf_op jit(solution)/shard_map/convert_element_type | solution.py:77
  942.8 0.0 copy-done
  942.8 81.1 %fusion.6 = bf16[128,180,256]{2,1,0:T(8,128)(2,1)} fusion(f32[8,16,180,256]{3,2,1,0:T(8,128)} %copy.40, bf16[128,4,180,3,196]{4,2,3,1,0:T(8,128)(2,1)} %copy.33, bf16[128,1,196,256]{3,2,1,0:T(8,128)(2,1)} %get-tuple-element.9, bf16[128,1,196,256]{3,2,1,0:T(8,128)(2,1)} %get-tuple-element.8, bf16[128,1,196,256]{3,2,1,0:T(8,128)(2,1)} %get-tuple-element.7, ...), kind=kOutput, calls=%fused_computation.10 | convolution fusion | flops 39910637568 | bytes 194625536 | tf_op jit(solution)/shard_map/ikjc,kcd->ijd/dot_general | solution.py:72
  1023.9 16.1 %copy.41 = bf16[128,180,256]{2,0,1:T(8,128)(2,1)} copy(bf16[128,180,256]{2,1,0:T(8,128)(2,1)} %fusion.6) | data formatting | bytes 23592960 | tf_op jit(solution)/shard_map/convert_element_type | solution.py:77
  (6 shorter events, 0.1 us)
Async XLA Ops:
  0.0 942.8 %copy-start = (bf16[4,256,256]{2,1,0:T(8,128)(2,1)S(1)}, bf16[4,256,256]{2,1,0:T(8,128)(2,1)}, u32[]{:S(2)}) copy-start(bf16[4,256,256]{2,1,0:T(8,128)(2,1)} %param.8) | copy-start | bytes 1572868
  13.9 5.9 copy-start.1
  13.9 265.0 %all-to-all-start = ((bf16[128,180,256]{2,1,0:T(8,128)(2,1)}), bf16[128,180,256]{2,1,0:T(8,128)(2,1)}, u32[]{:S(2)}, u32[]{:S(2)}) async-start(bf16[128,180,256]{2,1,0:T(8,128)(2,1)} %copy.26), calls=%async_computation | async-start | bytes 24117248 | tf_op jit(solution)/shard_map/all_to_all | solution.py:74
  40.4 251.8 %slice-start = ((s8[4423680]{0:T(1024)(128)(4,1)}), s8[229376]{0:T(1024)(128)(4,1)S(1)}, s32[]{:S(2)}) async-start(s8[4423680]{0:T(1024)(128)(4,1)} %bitcast.86), calls=%async_computation.2 | async-start | bytes 458752
  278.8 13.4 %slice-start.1 = ((s8[4423680]{0:T(1024)(128)(4,1)}), s8[4194304]{0:T(1024)(128)(4,1)S(1)}, s32[]{:S(2)}) async-start(s8[4423680]{0:T(1024)(128)(4,1)} %bitcast.86), calls=%async_computation.3 | async-start | bytes 8388608
  386.5 11.0 %copy-start.3 = (s32[128]{0:T(128)S(1)}, s32[128]{0:T(128)}, u32[]{:S(2)}) copy-start(s32[128]{0:T(128)} %param.7) | copy-start | bytes 1540
  386.5 11.1 %copy-start.2 = (f32[128,4,3,17]{0,1,3,2:T(4,128)S(1)}, f32[128,4,3,17]{0,1,3,2:T(4,128)}, u32[]{:S(2)}) copy-start(f32[128,4,3,17]{0,1,3,2:T(4,128)} %param.6) | copy-start | bytes 313348
  386.5 532.6 %all-to-all-start.1 = ((bf16[16,1440,256]{2,0,1:T(8,128)(2,1)}), bf16[16,1440,256]{2,0,1:T(8,128)(2,1)}, u32[]{:S(2)}, u32[]{:S(2)}) async-start(bf16[16,1440,256]{2,0,1:T(8,128)(2,1)} %copy.39), calls=%async_computation.1 | async-start | bytes 23592960 | tf_op jit(solution)/shard_map/all_to_all | solution.py:76
  395.0 262.9 %collective-permute-start.1 = (bf16[128,8,256]{2,1,0:T(8,128)(2,1)S(1)}, bf16[128,8,256]{2,1,0:T(8,128)(2,1)S(1)}, u32[]{:S(2)}, u32[]{:S(2)}) collective-permute-start(bf16[128,8,256]{2,1,0:T(8,128)(2,1)S(1)} %get-tuple-element.13), channel_id=1, source_target_pairs={{1,0},{2,1},{3,2},{4,3},{5,4},{6,5},{7,6},{0,7},{9,8},{10,9},{11,1... | collective-permute-start | bytes 1572872 | tf_op jit(solution)/shard_map/ppermute | solution.py:22
  395.4 262.7 %collective-permute-start = (bf16[128,8,256]{2,1,0:T(8,128)(2,1)S(1)}, bf16[128,8,256]{2,1,0:T(8,128)(2,1)S(1)}, u32[]{:S(2)}, u32[]{:S(2)}) collective-permute-start(bf16[128,8,256]{2,1,0:T(8,128)(2,1)S(1)} %get-tuple-element.12), channel_id=1, source_target_pairs={{0,1},{1,2},{2,3},{3,4},{4,5},{5,6},{6,7},{7,0},{8,9},{9,10},{10,1... | collective-permute-start | bytes 1572872 | tf_op jit(solution)/shard_map/ppermute | solution.py:19
  665.2 221.6 %collective-permute-start.2 = (bf16[1,196,256]{2,1,0:T(8,128)(2,1)S(1)}, bf16[1,196,256]{2,1,0:T(8,128)(2,1)S(1)}, u32[]{:S(2)}, u32[]{:S(2)}) collective-permute-start(bf16[1,196,256]{2,1,0:T(8,128)(2,1)S(1)} %get-tuple-element.10), channel_id=1, source_target_pairs={{0,8},{8,16},{16,24},{1,9},{9,17},{17,25},{2,10},{10,18},{18,26},{... | collective-permute-start | bytes 301064 | tf_op jit(solution)/shard_map/ppermute | solution.py:19
  670.8 216.1 %collective-permute-start.3 = (bf16[1,196,256]{2,1,0:T(8,128)(2,1)S(1)}, bf16[1,196,256]{2,1,0:T(8,128)(2,1)S(1)}, u32[]{:S(2)}, u32[]{:S(2)}) collective-permute-start(bf16[1,196,256]{2,1,0:T(8,128)(2,1)S(1)} %get-tuple-element.11), channel_id=1, source_target_pairs={{8,0},{16,8},{24,16},{9,1},{17,9},{25,17},{10,2},{18,10},{26,18},{... | collective-permute-start | bytes 301064 | tf_op jit(solution)/shard_map/ppermute | solution.py:22
where the time goes:
time: 1050 us; the launch traced here: 1040 us
  waiting for transfers between devices  499 us (48%)
  local copies, waits for them, and re-layouts  265 us (25%)
  matrix products  173 us (16%)
  other arithmetic  80.3 us (8%)
  starting transfers between devices  22.8 us (2%)
    ppermute x2, waiting for transfers between devices, with_halo(): lax.ppermute(lax.slice_in_dim(block, 0, width, axis=dim), axis, backward)  260 us
    all_to_all x1, waiting for transfers between devices, shards(): lax.all_to_all(fields, 'lon', split_axis=0, concat_axis=1, tiled=True)  238 us
    convert_element_type x1, local copies, waits for them, and re-layouts, shards(): band = jnp.einsum('ikab,jpb->ikjap', filters, select, preferred_element_t...  175 us
    dot_general x1, matrix products, shards(): jnp.einsum('ikjc,kcd->ijd', conv, mixing, preferred_element_type=jnp.floa...  81.1 us
    dot_general x1, matrix products, shards(): jnp.einsum('ikab,jpb->ikjap', filters, select, preferred_element_type=jnp...  39.5 us
    another operation x1, other arithmetic, shards(): jnp.stack([padded[0:lat_rows], padded[1:lat_rows + 1], padded[2:lat_rows...  32.2 us
    convert_element_type x1, local copies, waits for them, and re-layouts, transform(): jnp.einsum('rfc,nf->rnc', filtered, adjoint, preferred_element_type=jnp.f...  28.1 us
    dot_general x1, matrix products, transform(): jnp.einsum('rnc,nf->rfc', piece, forward, preferred_element_type=jnp.floa...  27.4 us
  transfers between devices with their start and end apart: 6, of which 3 were waited for; matrix products, arithmetic and copies ran while one was open for 27% of the time, Pallas kernels for 0%

commit v1 on v0

--- a/solution.py
+++ b/solution.py
@@ -71,7 +71,10 @@
     )
     local = jnp.einsum("ikjc,kcd->ijd", conv, mixing, preferred_element_type=jnp.float32)
     forward, adjoint = make_tables(NLON, MODES)
-    gathered = lax.all_to_all(fields, "lon", split_axis=0, concat_axis=1, tiled=True)
+    gathered = jnp.concatenate(
+        lax.all_to_all(jnp.stack(jnp.split(fields, lax.axis_size("lon"), axis=0)), "lon", 0, 0),
+        axis=1,
+    )
     result = transform(gathered, forward, adjoint, gains[0], gains[1])
     back = lax.all_to_all(result, "lon", split_axis=1, concat_axis=0, tiled=True)
     return (fields.astype(jnp.float32) + local + back.astype(jnp.float32)).astype(jnp.bfloat16)

time: 1050 us -> 788 us (0.75)
  waiting for transfers between devices: 499 us -> 231 us
  other arithmetic: 80.3 us -> 109 us
  local copies, waits for them, and re-layouts: 265 us -> 254 us
    all_to_all x1, waiting for transfers between devices: 238 us -> 0.01 us  [shards(): lax.all_to_all(jnp.stack(jnp.split(fields, lax.axis_size('lon'), axis=0))...]
    ppermute x2, waiting for transfers between devices: 260 us -> 231 us  [with_halo(): lax.ppermute(lax.slice_in_dim(block, 0, width, axis=dim), axis, backward)]
    convert_element_type x0 -> x1, other arithmetic: none -> 23.4 us  [shards(): (fields.astype(jnp.float32) + local + back.astype(jnp.float32)).astype(jn...]
    unnamed x13 -> x34, local copies, waits for them, and re-layouts: 13.9 us -> 30.4 us
    convert_element_type x1 -> x0, local copies, waits for them, and re-layouts: 16.1 us -> none  [shards(): (fields.astype(jnp.float32) + local + back.astype(jnp.float32)).astype(jn...]
    all_to_all x1 -> x0, local copies, waits for them, and re-layouts: 13.4 us -> none  [shards(): lax.all_to_all(fields, 'lon', split_axis=0, concat_axis=1, tiled=True)]
  transfers between devices with their start and end apart: 6 -> 6, of which waited for: 3 -> 1; matrix products, arithmetic and copies ran while one was open for 27% -> 58% of each run, Pallas kernels for 0% -> 0%
where the time goes in v1:
time: 788 us; the launch traced here: 779 us
  local copies, waits for them, and re-layouts  254 us (32%)
  waiting for transfers between devices  231 us (29%)
  matrix products  164 us (21%)
  other arithmetic  109 us (14%)
  starting transfers between devices  20.5 us (3%)
    ppermute x2, waiting for transfers between devices, with_halo(): lax.ppermute(lax.slice_in_dim(block, 0, width, axis=dim), axis, backward)  231 us
    convert_element_type x1, local copies, waits for them, and re-layouts, shards(): band = jnp.einsum('ikab,jpb->ikjap', filters, select, preferred_element_t...  175 us
    dot_general x1, matrix products, shards(): jnp.einsum('ikjc,kcd->ijd', conv, mixing, preferred_element_type=jnp.floa...  74.3 us
    dot_general x1, matrix products, shards(): jnp.einsum('ikab,jpb->ikjap', filters, select, preferred_element_type=jnp...  39.4 us
    another operation x1, other arithmetic, shards(): jnp.stack([padded[0:lat_rows], padded[1:lat_rows + 1], padded[2:lat_rows...  32.4 us
    unnamed x34, local copies, waits for them, and re-layouts  30.4 us
    convert_element_type x1, local copies, waits for them, and re-layouts, transform(): jnp.einsum('rfc,nf->rnc', filtered, adjoint, preferred_element_type=jnp.f...  28.2 us
    dot_general x1, matrix products, transform(): jnp.einsum('rnc,nf->rfc', piece, forward, preferred_element_type=jnp.floa...  26.3 us
  transfers between devices with their start and end apart: 6, of which 1 were waited for; matrix products, arithmetic and copies ran while one was open for 58% of the time, Pallas kernels for 0%

profile of v1, /device:TPU:13, one launch (start us, length us, event | category | flops | bytes accessed | tf_op | source)
XLA Modules:
  0.0 778.6 jit_solution(4508286108227091206)
XLA Ops:
  0.0 0.0 copy-start
  0.0 2.7 bitcast_dynamic-update-slice_fusion.7
  2.7 2.6 bitcast_dynamic-update-slice_fusion.6
  5.3 2.6 bitcast_dynamic-update-slice_fusion.5
  7.9 2.6 bitcast_dynamic-update-slice_fusion.4
  10.5 2.6 bitcast_dynamic-update-slice_fusion.3
  13.1 2.6 bitcast_dynamic-update-slice_fusion.2
  15.7 2.6 bitcast_dynamic-update-slice_fusion.1
  18.3 2.6 bitcast_dynamic-update-slice_fusion
  20.9 5.7 all-to-all-start
  26.5 0.0 copy-start.9
  26.5 0.0 copy-start.8
  26.5 0.0 copy-start.7
  26.5 12.1 %copy.14 = bf16[128,180,256]{2,1,0:T(8,128)(2,1)S(1)} copy(bf16[128,180,256]{2,0,1:T(8,128)(2,1)} %param.5) | data formatting | bytes 23592960 | tf_op args[0]
  38.6 0.0 copy-start.2
  38.6 0.2 fusion.41
  38.8 0.3 collective-permute-start.1
  39.2 2.1 collective-permute-start
  41.3 0.0 copy-done.9
  41.3 0.1 compare_convert_fusion
  41.3 0.0 copy-done.8
  41.4 0.0 copy-done.7
  41.4 0.1 slice_bitcast_fusion.1
  41.5 0.1 pad_maximum_fusion.8
  41.6 19.7 %sine_negate_fusion = (f32[1440,720]{0,1:T(8,128)}, f32[1440,720]{0,1:T(8,128)}) fusion(), kind=kLoop, calls=%fused_computation.40 | loop fusion | flops 10368000 | bytes 8294400 | tf_op jit(solution)/shard_map/neg | solution.py:34
  61.3 230.5 %collective-permute-done.1 = bf16[128,8,256]{2,1,0:T(8,128)(2,1)S(1)} collective-permute-done((bf16[128,8,256]{2,1,0:T(8,128)(2,1)S(1)}, bf16[128,8,256]{2,1,0:T(8,128)(2,1)S(1)}, u32[]{:S(2)}, u32[]{:S(2)}) %collective-permute-start.1) | collective-permute-done | bytes 524320 | tf_op jit(solution)/shard_map/ppermute | solution.py:22
  291.8 0.0 collective-permute-done
  291.8 0.0 copy-start.5
  291.8 3.0 pad_maximum_fusion.6
  294.8 0.0 copy-done.2
  294.8 0.0 copy-done.3
  294.8 0.0 copy-done.5
  294.8 0.7 fusion.40
  295.5 4.8 collective-permute-start.2
  300.3 2.4 collective-permute-start.3
  302.7 0.0 all-to-all-done
  302.8 26.3 %convolution_bitcast_fusion = f32[16,1440,256]{2,1,0:T(8,128)} fusion(bf16[16,1440,256]{2,0,1:T(8,128)(2,1)} %bitcast.27, f32[1440,720]{0,1:T(8,128)} %get-tuple-element.16, f32[1440,720]{0,1:T(8,128)} %get-tuple-element.17), kind=kOutput, calls=%fused_computation.13 | convolution fusion | flops 16995225600 | bytes 43683840 | tf_op jit(solution)/shard_map/rnc,nf->rfc/dot_general | solution.py:42
  329.0 13.8 %subtract_convert_fusion = (bf16[16,720,256]{2,1,0:T(8,128)(2,1)}, bf16[16,720,256]{2,1,0:T(8,128)(2,1)}) fusion(f32[16,1440,256]{2,1,0:T(8,128)} %convolution_bitcast_fusion, f32[720,256]{1,0:T(8,128)S(1)} %get-tuple-element.15, f32[720,256]{1,0:T(8,128)S(1)} %get-tuple-element.14), kind=kLoop, calls=%fused_computation.29 | loop fusion | flops 23592960 | bytes 36864000 | tf_op jit(solution)/shard_map/convert.3
  342.8 24.3 %fusion.13 = bf16[16,1440,256]{2,1,0:T(8,128)(2,1)S(1)} fusion(bf16[16,720,256]{2,1,0:T(8,128)(2,1)} %get-tuple-element.6, bf16[16,720,256]{2,1,0:T(8,128)(2,1)} %get-tuple-element.5, f32[1440,720]{0,1:T(8,128)} %get-tuple-element.16, f32[1440,720]{0,1:T(8,128)} %get-tuple-element.17, f32[1440]{0:T(1024)S(1)} %pad_maximum_fusion.8), kind=kOutput, calls=%fused_computation.30 | convolution fusion | flops 17022643200 | bytes 31893120 | tf_op jit(solution)/shard_map/rfc,nf->rnc/dot_general | solution.py:48
  367.2 28.2 %copy.23 = bf16[16,1440,256]{2,0,1:T(8,128)(2,1)} copy(bf16[16,1440,256]{2,1,0:T(8,128)(2,1)S(1)} %fusion.13) | data formatting | bytes 23592960 | tf_op jit(solution)/shard_map/convert_element_type | solution.py:48
  395.4 5.2 all-to-all-start.1
  400.6 39.4 %convert_bitcast_fusion = bf16[128,4,180,3,196]{0,4,3,1,2:T(8,128)(2,1)} fusion(s32[180,196]{1,0:T(8,128)S(1)} %iota_subtract_fusion, bf16[128,4,3,17]{0,1,3,2:T(4,128)(2,1)S(1)} %multiply_convert_fusion.1), kind=kOutput, calls=%fused_computation | convolution fusion | flops 1897252608 | bytes 108573504 | tf_op jit(solution)/shard_map/ikab,jpb->ikjap/dot_general | solution.py:65
  440.0 0.0 copy-start.4
  440.0 0.0 copy-start.6
  440.0 174.6 %copy.19 = bf16[128,4,180,3,196]{4,2,3,1,0:T(8,128)(2,1)} copy(bf16[128,4,180,3,196]{0,4,3,1,2:T(8,128)(2,1)} %convert_bitcast_fusion) | data formatting | bytes 216760320 | tf_op jit(solution)/shard_map/convert_element_type | solution.py:67
  614.6 0.0 collective-permute-done.2
  614.6 0.0 collective-permute-done.3
  614.6 0.0 copy-done.4
  614.6 0.0 copy-done.6
  614.6 32.4 %fusion.8 = (bf16[128,1,196,256]{3,2,1,0:T(8,128)(2,1)}, bf16[128,1,196,256]{3,2,1,0:T(8,128)(2,1)}, bf16[128,1,196,256]{3,2,1,0:T(8,128)(2,1)}) fusion(bf16[1,196,256]{2,1,0:T(8,128)(2,1)} %collective-permute-done.2, bf16[128,8,256]{2,1,0:T(8,128)(2,1)S(1)} %copy-done.4, bf16[128,180,256]{2,1,0:T(8,128)(2,1)} %copy-done.2, ...), kind=kLoop, calls=%fused_computation.20 | loop fusion | flops 141295616 | bytes 51580928 | tf_op jit(solution)/shard_map/stack | solution.py:68
  647.0 0.0 copy-done
  647.0 74.3 %fusion = f32[128,180,256,1]{2,1,3,0:T(8,128)} fusion(bf16[128,4,180,3,196]{4,2,3,1,0:T(8,128)(2,1)} %copy.19, bf16[128,1,196,256]{3,2,1,0:T(8,128)(2,1)} %get-tuple-element.9, bf16[128,1,196,256]{3,2,1,0:T(8,128)(2,1)} %get-tuple-element.8, bf16[128,1,196,256]{3,2,1,0:T(8,128)(2,1)} %get-tuple-element.7, bf16[4,256,256]{2,1,0:T(8,128)(2,1)S(1)} %copy-done), kind=kOutput, calls=%fused_computation.2 | convolution fusion | flops 39887044608 | bytes 171032576 | tf_op jit(solution)/shard_map/ikjc,kcd->ijd/dot_general | solution.py:72
  721.3 0.0 all-to-all-done.1
  721.3 0.0 slice-start
  721.3 0.0 slice-start.1
  721.3 16.3 %convert_bitcast_fusion.1 = f32[8,16,180,256]{3,1,2,0:T(8,128)} fusion(bf16[16,8,180,256]{3,0,2,1:T(8,128)(2,1)} %bitcast.39), kind=kLoop, calls=%fused_computation.9 | loop fusion | flops 5898240 | bytes 35389440 | tf_op jit(solution)/shard_map/convert_element_type | solution.py:80
  737.6 0.0 slice-start.2
  737.6 17.4 %copy.24 = f32[8,16,180,256]{3,1,0,2:T(8,128)} copy(f32[8,16,180,256]{3,1,2,0:T(8,128)} %convert_bitcast_fusion.1) | data formatting | bytes 47185920 | tf_op jit(solution)/shard_map/convert_element_type | solution.py:80
  755.0 0.0 slice-done
  755.0 0.0 slice-done.1
  755.0 0.0 slice-done.2
  755.0 0.0 copy-start.1
  755.0 23.4 %fusion.6 = bf16[128,180,256]{2,0,1:T(8,128)(2,1)} fusion(f32[8,16,180,256]{3,1,0,2:T(8,128)} %copy.24, f32[128,180,256,1]{2,1,3,0:T(8,128)} %fusion, bf16[128,180,256]{2,0,1:T(8,128)(2,1)S(1)} %bitcast.94), kind=kLoop, calls=%fused_computation.11 | loop fusion | flops 23592960 | bytes 70778880 | tf_op jit(solution)/shard_map/convert_element_type | solution.py:80
  778.4 0.0 copy-done.1
  (6 shorter events, 0.1 us)
Async XLA Ops:
  0.0 647.0 %copy-start = (bf16[4,256,256]{2,1,0:T(8,128)(2,1)S(1)}, bf16[4,256,256]{2,1,0:T(8,128)(2,1)}, u32[]{:S(2)}) copy-start(bf16[4,256,256]{2,1,0:T(8,128)(2,1)} %param.8) | copy-start | bytes 1572868
  20.9 281.9 %all-to-all-start = ((bf16[8,16,180,256]{3,1,2,0:T(8,128)(2,1)}), bf16[8,16,180,256]{3,1,2,0:T(8,128)(2,1)}, u32[]{:S(2)}, u32[]{:S(2)}) async-start(bf16[8,16,180,256]{3,1,2,0:T(8,128)(2,1)} %bitcast_dynamic-update-slice_fusion), calls=%async_computation | async-start | bytes 23592960 | tf_op jit(solution)/shard_map/all_to_all | solution.py:75
  26.5 14.7 %copy-start.9 = (s32[128]{0:T(128)S(1)}, s32[128]{0:T(128)}, u32[]{:S(2)}) copy-start(s32[128]{0:T(128)} %param.7) | copy-start | bytes 1540
  26.5 14.8 %copy-start.8 = (f32[128,4,3,17]{0,1,3,2:T(4,128)S(1)}, f32[128,4,3,17]{0,1,3,2:T(4,128)}, u32[]{:S(2)}) copy-start(f32[128,4,3,17]{0,1,3,2:T(4,128)} %param.6) | copy-start | bytes 313348
  26.5 14.8 %copy-start.7 = (f32[2,720,256]{2,1,0:T(8,128)S(1)}, f32[2,720,256]{2,1,0:T(8,128)}, u32[]{:S(2)}) copy-start(f32[2,720,256]{2,1,0:T(8,128)} %param.9) | copy-start | bytes 4423684
  38.6 256.2 %copy-start.2 = (bf16[128,180,256]{2,1,0:T(8,128)(2,1)}, bf16[128,180,256]{2,1,0:T(8,128)(2,1)S(1)}, u32[]{:S(2)}) copy-start(bf16[128,180,256]{2,1,0:T(8,128)(2,1)S(1)} %copy.14) | copy-start | bytes 35389444
  38.8 253.0 %collective-permute-start.1 = (bf16[128,8,256]{2,1,0:T(8,128)(2,1)S(1)}, bf16[128,8,256]{2,1,0:T(8,128)(2,1)S(1)}, u32[]{:S(2)}, u32[]{:S(2)}) collective-permute-start(bf16[128,8,256]{2,1,0:T(8,128)(2,1)S(1)} %get-tuple-element.13), channel_id=1, source_target_pairs={{1,0},{2,1},{3,2},{4,3},{5,4},{6,5},{7,6},{0,7},{9,8},{10,9},{11,1... | collective-permute-start | bytes 1572872 | tf_op jit(solution)/shard_map/ppermute | solution.py:22
  39.2 252.7 %collective-permute-start = (bf16[128,8,256]{2,1,0:T(8,128)(2,1)S(1)}, bf16[128,8,256]{2,1,0:T(8,128)(2,1)S(1)}, u32[]{:S(2)}, u32[]{:S(2)}) collective-permute-start(bf16[128,8,256]{2,1,0:T(8,128)(2,1)S(1)} %get-tuple-element.12), channel_id=1, source_target_pairs={{0,1},{1,2},{2,3},{3,4},{4,5},{5,6},{6,7},{7,0},{8,9},{9,10},{10,1... | collective-permute-start | bytes 1572872 | tf_op jit(solution)/shard_map/ppermute | solution.py:19
  291.8 3.0 copy-start.3
  291.8 3.0 copy-start.5
  295.5 319.1 %collective-permute-start.2 = (bf16[1,196,256]{2,1,0:T(8,128)(2,1)}, bf16[1,196,256]{2,1,0:T(8,128)(2,1)}, u32[]{:S(2)}, u32[]{:S(2)}) collective-permute-start(bf16[1,196,256]{2,1,0:T(8,128)(2,1)} %get-tuple-element.10), channel_id=1, source_target_pairs={{0,8},{8,16},{16,24},{1,9},{9,17},{17,25},{2,10},{10,18},{18,26},{... | collective-permute-start | bytes 301064 | tf_op jit(solution)/shard_map/ppermute | solution.py:19
  300.3 314.2 %collective-permute-start.3 = (bf16[1,196,256]{2,1,0:T(8,128)(2,1)}, bf16[1,196,256]{2,1,0:T(8,128)(2,1)}, u32[]{:S(2)}, u32[]{:S(2)}) collective-permute-start(bf16[1,196,256]{2,1,0:T(8,128)(2,1)} %get-tuple-element.11), channel_id=1, source_target_pairs={{8,0},{16,8},{24,16},{9,1},{17,9},{25,17},{10,2},{18,10},{26,18},{... | collective-permute-start | bytes 301064 | tf_op jit(solution)/shard_map/ppermute | solution.py:22
  395.4 325.9 %all-to-all-start.1 = ((bf16[16,1440,256]{2,0,1:T(8,128)(2,1)}), bf16[16,1440,256]{2,0,1:T(8,128)(2,1)}, u32[]{:S(2)}, u32[]{:S(2)}) async-start(bf16[16,1440,256]{2,0,1:T(8,128)(2,1)} %copy.23), calls=%async_computation.1 | async-start | bytes 23592960 | tf_op jit(solution)/shard_map/all_to_all | solution.py:79
  440.0 174.6 %copy-start.4 = (bf16[128,8,256]{2,1,0:T(8,128)(2,1)S(1)}, bf16[128,8,256]{2,1,0:T(8,128)(2,1)}, u32[]{:S(2)}) copy-start(bf16[128,8,256]{2,1,0:T(8,128)(2,1)} %copy-done.3) | copy-start | bytes 1572868
  440.0 174.6 %copy-start.6 = (bf16[128,8,256]{2,1,0:T(8,128)(2,1)S(1)}, bf16[128,8,256]{2,1,0:T(8,128)(2,1)}, u32[]{:S(2)}) copy-start(bf16[128,8,256]{2,1,0:T(8,128)(2,1)} %copy-done.5) | copy-start | bytes 1572868
  721.3 33.7 %slice-start = ((s8[11796480]{0:T(1024)(128)(4,1)}), s8[4194304]{0:T(1024)(128)(4,1)S(1)}, s32[]{:S(2)}) async-start(s8[11796480]{0:T(1024)(128)(4,1)} %bitcast.93), calls=%async_computation.2 | async-start | bytes 8388608
  721.3 33.7 %slice-start.1 = ((s8[11796480]{0:T(1024)(128)(4,1)}), s8[4194304]{0:T(1024)(128)(4,1)S(1)}, s32[]{:S(2)}) async-start(s8[11796480]{0:T(1024)(128)(4,1)} %bitcast.93), calls=%async_computation.3 | async-start | bytes 8388608
  737.6 17.4 %slice-start.2 = ((s8[11796480]{0:T(1024)(128)(4,1)}), s8[3407872]{0:T(1024)(128)(4,1)S(1)}, s32[]{:S(2)}) async-start(s8[11796480]{0:T(1024)(128)(4,1)} %bitcast.93), calls=%async_computation.4 | async-start | bytes 6815744
  755.0 23.4 %copy-start.1 = (bf16[4,256,256]{2,1,0:T(8,128)(2,1)S(1)}, bf16[4,256,256]{2,1,0:T(8,128)(2,1)}, u32[]{:S(2)}) copy-start(bf16[4,256,256]{2,1,0:T(8,128)(2,1)} %param.8) | copy-start | bytes 1572868
